TPU v7x, 256 devices: a whole 4x4x8 slice. The times are simulated.
256 devices in a mesh: grp: 2 (over core), row: 16 (over y, z_hi), col: 8 (over x, z_lo).
Axes of the slice: x: 4, y: 4, z: 8 (z_hi: 4, z_lo: 2; z = z_hi * 2 + z_lo), core: 2. Of those that a mesh axis runs over, the one named last changes fastest.
Arguments:
- tokens: bfloat16 [1024, 16384], P('col', ('grp', 'row')), may hold values from -48 to 48
- norm_gain: bfloat16 [16384], P(('grp', 'row')), may hold values from 0.099609375 to 1.8984375
- query_weight: bfloat16 [16384, 16384], P(('grp', 'row'), 'col'), may hold values from -24 to 24
- key_weight: bfloat16 [16384, 1024], P(('grp', 'row'), 'col'), may hold values from -1 to 1
- value_weight: bfloat16 [16384, 1024], P(('grp', 'row'), 'col'), may hold values from -0.046875 to 0.046875
- output_weight: bfloat16 [16384, 16384], P('col', ('grp', 'row')), may hold values from -0.046875 to 0.046875
Outputs:
- gram: float32 [16384, 16384], P('col', ('grp', 'row'))
- cross: float32 [16384, 16384], P('col', ('grp', 'row'))
All inputs are finite; a program needn't handle non-finite values.
Results may differ from a plain program's by a relative error of at most 0.015.
Values may be sent and summed in bfloat16 or wider, within the bound.
A program may use at most 128 MiB of HBM per device.

v0:
```python
import math

import jax
import jax.numpy as jnp
from jax import lax
from jax.sharding import PartitionSpec as P

D = 16384
H = 128
KVH = 8
HD = 128


def rotate(values, positions):
    half = values.shape[-1] // 2
    frequency = 500000.0 ** (-jnp.arange(half, dtype=jnp.float32) * 2.0 / values.shape[-1])
    angles = positions[:, None] * frequency[None, :]
    cosine = jnp.cos(angles)[:, None, :]
    sine = jnp.sin(angles)[:, None, :]
    first = values[..., :half]
    second = values[..., half:]
    return jnp.concatenate(
        [first * cosine - second * sine, second * cosine + first * sine], axis=-1
    )


def panel_product(left, right):
    return lax.dot_general(
        left, right, (((0,), (0,)), ((), ())), preferred_element_type=jnp.float32
    )


def per_device(tokens, norm_gain, query_weight, key_weight, value_weight, output_weight):
    wide = tokens.astype(jnp.float32)
    squares = lax.psum(jnp.sum(wide * wide, axis=1), ("grp", "row"))
    normed = (
        wide * lax.rsqrt(squares / D + 1e-05)[:, None] * norm_gain.astype(jnp.float32)[None, :]
    ).astype(jnp.bfloat16)
    gathered, gathered_normed = (
        lax.all_gather(tokens, "col", axis=0, tiled=True),
        lax.all_gather(normed, "col", axis=0, tiled=True),
    )
    seq_len = gathered.shape[0]
    feature_groups = lax.axis_size(("grp", "row"))
    query_rows = seq_len // feature_groups
    query_cols = query_weight.shape[1]
    key_cols = key_weight.shape[1]
    local_heads = query_cols // HD
    local_kv = key_cols // HD
    first_row = lax.axis_index(("grp", "row")) * query_rows
    positions = (first_row + jnp.arange(query_rows, dtype=jnp.int32)).astype(jnp.float32)
    joined_weight = jnp.concatenate([query_weight, key_weight, value_weight], axis=1)
    projected = lax.psum_scatter(
        jnp.dot(gathered_normed, joined_weight, preferred_element_type=jnp.float32),
        ("grp", "row"),
        scatter_dimension=0,
        tiled=True,
    )
    queries = rotate(
        projected[:, :query_cols].reshape(query_rows, local_heads, HD), positions
    ).astype(jnp.bfloat16)
    keys = rotate(
        projected[:, query_cols : query_cols + key_cols].reshape(query_rows, local_kv, HD),
        positions,
    )
    keys = keys.astype(jnp.bfloat16).reshape(query_rows, key_cols)
    values = projected[:, query_cols + key_cols :].astype(jnp.bfloat16)
    all_keys, all_values = (
        lax.all_gather(keys, ("grp", "row"), axis=0, tiled=True),
        lax.all_gather(values, ("grp", "row"), axis=0, tiled=True),
    )
    grouped = queries.reshape(query_rows, local_kv, H // KVH, HD)
    key_heads = all_keys.reshape(seq_len, local_kv, HD)
    value_heads = all_values.reshape(seq_len, local_kv, HD)
    scores = jnp.einsum(
        "tkgd,skd->kgts", grouped, key_heads, preferred_element_type=jnp.float32
    ) / math.sqrt(HD)
    key_positions = jnp.arange(seq_len, dtype=jnp.int32)
    query_positions = first_row + jnp.arange(query_rows, dtype=jnp.int32)
    causal = key_positions[None, :] <= query_positions[:, None]
    scores = jnp.where(causal[None, None], scores, jnp.float32(-1e30))
    probs = jax.nn.softmax(scores, axis=-1).astype(jnp.bfloat16)
    attended = jnp.einsum("kgts,skd->tkgd", probs, value_heads, preferred_element_type=jnp.float32)
    attended = attended.astype(jnp.bfloat16).reshape(query_rows, query_cols)
    partial_branch = jnp.dot(
        lax.all_gather(attended, ("grp", "row"), axis=0, tiled=True),
        output_weight,
        preferred_element_type=jnp.float32,
    )
    branch = lax.psum(partial_branch, "col").astype(jnp.bfloat16)
    full_rows = lax.all_gather(tokens, ("grp", "row"), axis=1, tiled=True)
    panel_tokens = lax.all_to_all(full_rows, "col", split_axis=1, concat_axis=0, tiled=True)
    gram = panel_product(panel_tokens, gathered) / seq_len
    cross = panel_product(panel_tokens, branch) / seq_len
    return (gram, cross)


def solution(mesh):
    return jax.shard_map(
        per_device,
        mesh=mesh,
        in_specs=(
            P("col", ("grp", "row")),
            P(("grp", "row")),
            P(("grp", "row"), "col"),
            P(("grp", "row"), "col"),
            P(("grp", "row"), "col"),
            P("col", ("grp", "row")),
        ),
        out_specs=(P("col", ("grp", "row")), P("col", ("grp", "row"))),
        check_vma=False,
    )
```

profile of v0, /device:TPU:1, one launch (start us, length us, event | category | flops | bytes accessed | tf_op | source)
XLA Modules:
  0.0 609.8 jit_solution(338686081858578538)
XLA Ops:
  7.2 0.0 copy-start
  7.2 0.0 all-gather.9.cloned.1.call-start
  7.2 0.8 convert_element_type.40
  8.0 1.0 fusion.10
  9.1 79.7 %psum.14 = f32[128]{0:T(128)S(1)} all-reduce(f32[128]{0:T(128)S(1)} %fusion.10), channel_id=1, replica_groups=mesh['grp'=2,'row'=16,'col'=8] {'grp','row'}, use_global_device_ids=true, to_apply=%region_1.0 | all-reduce | flops 128 | bytes 1024 | tf_op jit(solution)/shard_map/psum | solution.py:35
  88.8 1.7 fusion.12
  90.5 0.0 all-gather.9.cloned.1.call-update
  90.5 0.0 reduce-scatter.2.cloned.1.call-start
  90.5 32.9 %all-gather.9.cloned.1.call-done = bf16[1024,512]{1,0:T(8,128)(2,1)} async-done(((bf16[128,512]{1,0:T(8,128)(2,1)}), bf16[1024,512]{1,0:T(8,128)(2,1)}) %all-gather.9.cloned.1.call-update) | async-done | bytes 1048592 | tf_op jit(solution)/shard_map/all_gather | solution.py:41
  123.5 8.3 %fusion = f32[1024,2304]{1,0:T(8,128)} fusion(bf16[1024,512]{1,0:T(8,128)(2,1)} %all-gather.9.cloned.1.call-done, bf16[512,128]{1,0:T(8,128)(2,1)} %param.10, bf16[512,128]{1,0:T(8,128)(2,1)} %param.9, bf16[512,2048]{1,0:T(8,128)(2,1)} %param.8), kind=kOutput, calls=%fused_computation.2 | convolution fusion | flops 2422996992 | bytes 12845056 | tf_op jit(solution)/shard_map/dot_general | solution.py:54
  131.7 0.0 copy-start.1
  131.7 0.0 reduce-scatter.2.cloned.1.call-update
  131.7 0.0 all-gather.5.cloned.1.call-start
  131.8 0.8 copy-done.1
  132.6 0.8 copy.15
  133.4 0.0 all-gather.5.cloned.1.call-update
  133.4 0.0 all-gather.7.cloned.1.call-start
  133.5 0.5 all-gather.7.cloned.1.call-update
  134.0 0.0 all-gather.11.cloned.1.call-start
  134.1 0.1 iota_compare_fusion
  134.2 0.1 multiply_cosine_fusion
  134.3 127.1 %reduce-scatter.2.cloned.1.call-done = f32[32,2304]{1,0:T(8,128)} async-done(((f32[1024,2304]{1,0:T(8,128)}), f32[32,2304]{1,0:T(8,128)}) %reduce-scatter.2.cloned.1.call-update) | async-done | bytes 294928 | tf_op jit(solution)/shard_map/reduce_scatter | solution.py:53
  261.4 1.0 slice_bitcast_fusion
  262.4 0.7 slice_bitcast_fusion.1
  263.1 0.1 fusion.27
  263.3 0.7 slice.51
  264.1 0.1 pad_maximum_fusion
  264.1 77.5 %all_gather.22 = bf16[1024,128]{1,0:T(8,128)(2,1)S(1)} all-gather(bf16[32,128]{1,0:T(8,128)(2,1)S(1)} %pad_maximum_fusion), channel_id=1, replica_groups=mesh['grp'=2,'row'=16,'col'=8] {'grp','row'}, dimensions={0}, use_global_device_ids=true | all-gather | bytes 270336 | tf_op jit(solution)/shard_map/all_gather | solution.py:69
  341.6 70.0 %all_gather.21 = bf16[1024,128]{1,0:T(8,128)(2,1)S(1)} all-gather(bf16[32,128]{1,0:T(8,128)(2,1)S(1)} %slice.51), channel_id=1, replica_groups=mesh['grp'=2,'row'=16,'col'=8] {'grp','row'}, dimensions={0}, use_global_device_ids=true | all-gather | bytes 270336 | tf_op jit(solution)/shard_map/all_gather | solution.py:70
  411.6 0.1 fusion.31
  411.7 0.2 subtract_convert_fusion
  411.9 0.6 fusion.32
  412.5 0.5 fusion.6
  413.0 0.5 fusion.7
  413.6 0.1 copy.19
  413.6 0.7 copy.30
  414.3 0.0 all-gather.11.cloned.1.call-update
  414.3 0.0 all-gather.5.cloned.1.call-done
  414.3 75.2 %all_to_all.19 = bf16[128,8,2048]{0,2,1:T(8,128)(2,1)} all-to-all(bf16[128,8,2048]{0,2,1:T(8,128)(2,1)} %bitcast.49), channel_id=1, replica_groups=mesh['grp'=2,'row'=16,'col'=8] {'col'}, dimensions={1} | all-to-all | bytes 8388608 | tf_op jit(solution)/shard_map/all_to_all | solution.py:92
  489.6 6.4 %copy.16 = bf16[8,128,2048]{2,1,0:T(8,128)(2,1)} copy(bf16[8,128,2048]{1,2,0:T(8,128)(2,1)} %bitcast.48) | data formatting | bytes 8388608 | tf_op jit(solution)/shard_map/all_to_all | solution.py:92
  496.0 0.0 all-gather.7.cloned.1.call-done
  496.0 6.9 %convolution_multiply_fusion = f32[2048,512]{1,0:T(8,128)} fusion(bf16[1024,2048]{1,0:T(8,128)(2,1)} %bitcast.46, bf16[1024,512]{1,0:T(8,128)(2,1)} %all-gather.7.cloned.1.call-done), kind=kOutput, calls=%fused_computation.1 | convolution fusion | flops 2148532224 | bytes 9437184 | tf_op jit(solution)/shard_map/dot_general | solution.py:28
  502.9 0.0 all-gather.11.cloned.1.call-done
  502.9 0.0 copy-done
  502.9 5.8 fusion.33
  508.7 82.7 %all-reduce.1 = bf16[1024,512]{1,0:T(8,128)(2,1)S(1)} all-reduce(f32[1024,512]{1,0:T(8,128)} %fusion.33), channel_id=1, replica_groups=mesh['grp'=2,'row'=16,'col'=8] {'col'}, use_global_device_ids=true, to_apply=%region_5.6 | all-reduce | flops 524288 | bytes 3145728 | tf_op jit(solution)/shard_map/psum | solution.py:90
  591.4 6.5 %multiply_bitcast_fusion = f32[2048,512]{0,1:T(8,128)} fusion(bf16[1024,2048]{1,0:T(8,128)(2,1)} %bitcast.47, bf16[1024,512]{1,0:T(8,128)(2,1)S(1)} %all-reduce.1), kind=kOutput, calls=%fused_computation | convolution fusion | flops 2148532224 | bytes 9437184 | tf_op jit(solution)/shard_map/dot_general | solution.py:28
  597.9 5.3 copy.20
  (5 shorter events, 0.1 us)
Async XLA Ops:
  7.2 495.7 %copy-start = (bf16[2048,512]{1,0:T(8,128)(2,1)S(1)}, bf16[2048,512]{1,0:T(8,128)(2,1)}, u32[]{:S(2)}) copy-start(bf16[2048,512]{1,0:T(8,128)(2,1)} %param.11) | copy-start | bytes 6291460
  7.2 116.3 %all-gather.9.cloned.1.call-start = ((), (), s32[]{:S(2)}) async-start(), calls=%async_computation.4 | async-start | bytes 1179648 | tf_op jit(solution)/shard_map/all_gather | solution.py:41
  90.5 170.9 %reduce-scatter.2.cloned.1.call-start = ((), (), s32[]{:S(2)}) async-start(), calls=%async_computation.5 | async-start | bytes 9732096 | tf_op jit(solution)/shard_map/reduce_scatter | solution.py:53
  131.7 0.9 copy-start.1
  131.7 282.6 %all-gather.5.cloned.1.call-start = ((), (), s32[]{:S(2)}) async-start(), calls=%async_computation.2 | async-start | bytes 4325376 | tf_op jit(solution)/shard_map/all_gather | solution.py:91
  133.4 362.6 %all-gather.7.cloned.1.call-start = ((), (), s32[]{:S(2)}) async-start(), calls=%async_computation.3 | async-start | bytes 1179648 | tf_op jit(solution)/shard_map/all_gather | solution.py:40
  134.0 368.9 %all-gather.11.cloned.1.call-start = ((), (), s32[]{:S(2)}) async-start(), calls=%async_computation.6 | async-start | bytes 4325376 | tf_op jit(solution)/shard_map/all_gather | solution.py:86
Sparse Core Ops, SparseCore 0:
  90.6 32.7 all-gather.8
  131.9 129.5 reduce-scatter.1
  264.9 61.2 all-gather.4
  328.0 35.8 all-gather.6
  414.4 66.1 all-gather.10
where the time goes:
time: 614 us; the launch traced here: 610 us
  blocking collectives  385 us (63%)
  waiting for transfers between devices  161 us (26%)
  matrix products  28.6 us (5%)
  local copies, waits for them, and re-layouts  16.7 us (3%)
  between operations  13.9 us (2%)
    reduce_scatter x1, waiting for transfers between devices, per_device(): lax.psum_scatter(jnp.dot(gathered_normed, joined_weight, preferred_elemen...  127 us
    psum x1, blocking collectives, per_device(): branch = lax.psum(partial_branch, 'col').astype(jnp.bfloat16)  82.7 us
    psum x1, blocking collectives, per_device(): squares = lax.psum(jnp.sum(wide * wide, axis=1), ('grp', 'row'))  79.7 us
    all_gather x1, blocking collectives, per_device(): lax.all_gather(keys, ('grp', 'row'), axis=0, tiled=True)  77.5 us
    all_to_all x1, blocking collectives, per_device(): lax.all_to_all(full_rows, 'col', split_axis=1, concat_axis=0, tiled=True)  75.2 us
    all_gather x1, blocking collectives, per_device(): lax.all_gather(values, ('grp', 'row'), axis=0, tiled=True)  70 us
    all_gather x1, waiting for transfers between devices, per_device(): lax.all_gather(normed, 'col', axis=0, tiled=True)  32.9 us
    dot_general x2, matrix products, panel_product(): lax.dot_general(left, right, (((0,), (0,)), ((), ())), preferred_element_...  13.4 us
  transfers between devices with their start and end apart: 5, of which 2 were waited for; matrix products, arithmetic and copies ran while one was open for 3% of the time, Pallas kernels for 0%

commit v1 on v0

v1 whole, which is shorter than its diff:
```python
import functools
import math

import jax
import jax.numpy as jnp
import numpy as np
from jax import lax
from jax.experimental import pallas as pl
from jax.experimental.pallas import tpu as pltpu
from jax.sharding import PartitionSpec as P

D = 16384
H = 128
HD = 128
LEN = 1024
MESH = pl.DeviceIdType.MESH
BF = jnp.bfloat16
F32 = jnp.float32
FB = 512
KVW = 384
QW = 1024
WIDTHS = (KVW, QW, QW)


def tables():
    half = HD // 2
    frequency = np.float32(500000.0) ** (-np.arange(half, dtype=np.float32) * np.float32(2.0 / HD))
    angles = np.arange(LEN, dtype=np.float32)[:, None] * frequency.astype(np.float32)[None, :]
    cosine = np.cos(angles.astype(np.float64)).astype(np.float32)
    sine = np.sin(angles.astype(np.float64)).astype(np.float32)
    return (
        np.concatenate([cosine, cosine], axis=1),
        np.concatenate([-sine, sine], axis=1),
    )


def strips(rows, step, body):
    def one(i, carry):
        body(pl.multiple_of(i * step, step))
        return carry

    lax.fori_loop(0, rows // step, one, 0)


def kernel(tok, gain, wk_in, wv_in, wq_in, wo_in, cos_in, sin_in, tf_out, panel_out, branch_out, *scratch):
    names = iter(scratch)
    nxt = lambda: next(names)
    tf, xg, sq, wkv, wq, wo, cosv, sinv = [nxt() for _ in range(8)]
    sib_send = [nxt() for _ in range(3)]
    sib_recv = [nxt() for _ in range(3)]
    r1 = [nxt() for _ in range(3)]
    y_send_p = [nxt() for _ in range(3)]
    y_send_m = [nxt() for _ in range(3)]
    y_send_f = [nxt() for _ in range(3)]
    y_recv_p = [nxt() for _ in range(3)]
    y_recv_m = [nxt() for _ in range(3)]
    y_recv_f = [nxt() for _ in range(3)]
    s2 = [nxt() for _ in range(3)]
    z_send = [nxt() for _ in range(3)]
    z_recv = [nxt() for _ in range(3)]
    kv, rs_scale, qs = [nxt() for _ in range(3)]
    att = [nxt() for _ in range(2)]
    acc, bsend, brecv, ball, panel = [nxt() for _ in range(5)]
    ssem, rsem, lsem, bssem, brsem = [nxt() for _ in range(5)]

    g = lax.axis_index("grp")
    row = lax.axis_index("row")
    c = lax.axis_index("col")
    y, zh = row // 4, row % 4
    x, zl = c // 2, c % 2

    def at_y(d):
        return {"row": ((y + d) % 4) * 4 + zh}

    def at_z(d):
        return {"row": y * 4 + (zh + d) % 4}

    def at_col(dx, dl):
        return {"col": ((x + dx) % 4) * 2 + (zl + dl) % 2}

    sibling = {"grp": 1 - g}
    col_offsets = [(0, 1), (1, 0), (3, 0), (1, 1), (3, 1), (2, 0), (2, 1)]

    local = []

    def load(src, dst):
        copy = pltpu.make_async_copy(src, dst, lsem.at[len(local)])
        copy.start()
        local.append(copy)
        return copy

    own_row = pl.multiple_of(g * 512 + y * 128 + zh * 32, 32)
    my_tokens = pl.ds(pl.multiple_of(c * 128, 128), 128)
    l_tok = load(tok, tf.at[my_tokens])
    l_k = load(wk_in, wkv.at[:, pl.ds(0, HD)])
    l_v = load(wv_in, wkv.at[:, pl.ds(HD, HD)])
    l_q = load(wq_in, wq)
    l_cos = load(cos_in.at[pl.ds(own_row, 32)], cosv)
    l_sin = load(sin_in.at[pl.ds(own_row, 32)], sinv)
    l_o = load(wo_in, wo)

    barrier = pltpu.get_barrier_semaphore()
    peers = [sibling] + [at_y(d) for d in (1, 2, 3)] + [at_z(d) for d in (1, 2, 3)]
    peers += [at_col(*o) for o in col_offsets]
    for peer in peers:
        pl.semaphore_signal(barrier, inc=1, device_id=peer, device_id_type=MESH)
    pl.semaphore_wait(barrier, len(peers))

    sends = []
    count = [0]

    def describe(src, dst, dev, index=None):
        if index is None:
            index = count[0]
            count[0] += 1
        return pltpu.make_async_remote_copy(
            src_ref=src,
            dst_ref=dst,
            send_sem=ssem.at[index],
            recv_sem=rsem.at[index],
            device_id=dev,
            device_id_type=MESH,
        )

    def send(src, dst, dev):
        copy = describe(src, dst, dev)
        copy.start()
        sends.append(copy)
        return copy

    gather = [send(tok, tf.at[my_tokens], at_col(*o)) for o in col_offsets]
    l_tok.wait()
    for copy in gather:
        copy.wait_recv()

    panel_core = g == c // 4
    delta = (y - c % 4 + 4) % 4
    is_source = jnp.logical_and(panel_core, delta == 0)
    part_a = [describe(tf, panel.at[zh], at_z(d)) for d in (1, 2, 3)]
    own_panel = pltpu.make_async_copy(tf, panel.at[zh], lsem.at[len(local)])
    local.append(None)

    @pl.when(is_source)
    def _():
        for copy in part_a:
            copy.start()
        own_panel.start()

    out_tf = pltpu.make_async_copy(tf, tf_out, lsem.at[len(local)])
    local.append(None)
    out_tf.start()

    def prepare(i):
        rows = pl.ds(i, 32)
        wide = tf[rows, :].astype(F32)
        xg[rows, :] = (wide * gain[...].astype(F32)).astype(BF)
        square = wide * wide
        sq[rows, :] = square[:, 0:128] + square[:, 128:256] + square[:, 256:384] + square[:, 384:512]

    strips(LEN, 32, prepare)

    mine = pl.multiple_of(g * 512, 512)
    theirs = pl.multiple_of((1 - g) * 512, 512)

    def project(k, base, out):
        weights, first, wide = (wkv, 0, 256) if k == 0 else (wq, (k - 1) * QW, QW)

        def tile(i):
            value = jnp.dot(
                xg[pl.ds(base, 512), :],
                weights[:, pl.ds(pl.multiple_of(first + i, 256), 256)],
                preferred_element_type=F32,
            )
            out[:, pl.ds(i, 256)] = value.astype(out.dtype)

        strips(wide, 256, tile)
        if k == 0:
            out[:, pl.ds(256, 128)] = sq[pl.ds(base, 512), :].astype(out.dtype)

    sib = [None] * 3

    def sib_stage(k):
        project(k, theirs, sib_send[k])
        sib[k] = send(sib_send[k], sib_recv[k], sibling)

    def own_stage(k):
        project(k, mine, r1[k])

    def y_rows(d):
        return pl.multiple_of(((y + d) % 4) * 128, 128)

    y_moves = [None] * 3

    def y_first(k):
        sib[k].wait_recv()

        def pair(d, dst, start, rows):
            base = y_rows(d)

            def strip(i):
                r = pl.ds(pl.multiple_of(base + start + i, 16), 16)
                dst[pl.ds(pl.multiple_of(start + i, 16), 16), :] = (r1[k][r, :] + sib_recv[k][r, :].astype(F32)).astype(BF)

            strips(rows, 16, strip)

        top, low = pl.ds(0, 64), pl.ds(64, 64)
        pair(2, y_send_f[k], 0, 128)
        m1p = send(y_send_f[k].at[top], y_recv_f[k].at[top], at_y(1))
        m1m = send(y_send_f[k].at[low], y_recv_f[k].at[low], at_y(3))
        pair(1, y_send_p[k], 64, 64)
        m2p = send(y_send_p[k].at[low], y_recv_p[k].at[low], at_y(1))
        pair(3, y_send_m[k], 0, 64)
        m2m = send(y_send_m[k].at[top], y_recv_m[k].at[top], at_y(3))
        y_moves[k] = [m1p, m1m, m2p, m2m]

    def y_second(k):
        top, low = pl.ds(0, 64), pl.ds(64, 64)
        m1p, m1m = y_moves[k][:2]

        def relay(d, dst, start):
            base = y_rows(d)

            def strip(i):
                r = pl.ds(pl.multiple_of(base + start + i, 16), 16)
                f = pl.ds(pl.multiple_of(start + i, 16), 16)
                dst[f, :] = (r1[k][r, :] + sib_recv[k][r, :].astype(F32) + y_recv_f[k][f, :].astype(F32)).astype(BF)

            strips(64, 16, strip)

        m1p.wait_recv()
        relay(1, y_send_p[k], 0)
        m3p = send(y_send_p[k].at[top], y_recv_p[k].at[top], at_y(1))
        m1m.wait_recv()
        relay(3, y_send_m[k], 64)
        m3m = send(y_send_m[k].at[low], y_recv_m[k].at[low], at_y(3))
        y_moves[k] += [m3p, m3m]

    z_moves = [None] * 3

    def z_first(k):
        for copy in y_moves[k][2:]:
            copy.wait_recv()
        base = y_rows(0)

        def strip(i):
            r = pl.ds(pl.multiple_of(base + i, 16), 16)
            f = pl.ds(i, 16)
            total = r1[k][r, :] + sib_recv[k][r, :].astype(F32) + y_recv_p[k][f, :].astype(F32) + y_recv_m[k][f, :].astype(F32)
            s2[k][f, :] = total
            z_send[k][f, :] = total.astype(BF)

        strips(128, 16, strip)
        z_moves[k] = [
            send(z_send[k].at[pl.ds(pl.multiple_of(((zh + d) % 4) * 32, 32), 32)], z_recv[k].at[d - 1], at_z(d))
            for d in (2, 1, 3)
        ]

    def z_sum(k, columns):
        own = pl.ds(pl.multiple_of(zh * 32, 32), 32)
        return (
            s2[k][own, columns]
            + z_recv[k][0, :, columns].astype(F32)
            + z_recv[k][1, :, columns].astype(F32)
            + z_recv[k][2, :, columns].astype(F32)
        )

    def rotated(values):
        return values * cosv[...] + pltpu.roll(values, 64, 1) * sinv[...]

    kv_moves = {}
    block_rows = pl.multiple_of(g * 512 + y * 128, 128)
    half_rows = pl.multiple_of(g * 512, 512)

    def kv_finish():
        for copy in z_moves[0]:
            copy.wait_recv()
        squares = jnp.sum(z_sum(0, pl.ds(256, 128)), axis=1, keepdims=True)
        scale = lax.rsqrt(squares / D + 1e-05)
        rs_scale[...] = jnp.broadcast_to(scale, (32, 128))
        l_cos.wait()
        l_sin.wait()
        rows = pl.ds(own_row, 32)
        kv[rows, pl.ds(0, HD)] = rotated(z_sum(0, pl.ds(0, HD)) * scale).astype(BF)
        kv[rows, pl.ds(HD, HD)] = (z_sum(0, pl.ds(HD, HD)) * scale).astype(BF)
        kv_moves["z"] = [send(kv.at[rows], kv.at[rows], at_z(d)) for d in (2, 1, 3)]

    def kv_y():
        for copy in kv_moves["z"]:
            copy.wait_recv()
        rows = pl.ds(block_rows, 128)
        kv_moves["y"] = [send(kv.at[rows], kv.at[rows], at_y(d)) for d in (2, 1, 3)]

    def kv_sib():
        for copy in kv_moves["y"]:
            copy.wait_recv()
        rows = pl.ds(half_rows, 512)
        kv_moves["s"] = send(kv.at[rows], kv.at[rows], sibling)

    att_moves = [{}, {}]

    def queries(k):
        for copy in z_moves[k]:
            copy.wait_recv()
        for h in range(8):
            value = z_sum(k, pl.ds(h * HD, HD)) * rs_scale[...]
            qs[k - 1, pl.ds(h * 32, 32), :] = rotated(value).astype(BF)

    def attention(k):
        n = 128
        for part in range(256 // n):
            scores = lax.dot_general(
                qs[k - 1, pl.ds(part * n, n), :], kv[:, pl.ds(0, HD)], (((1,), (1,)), ((), ())), preferred_element_type=F32
            ) * (1.0 / math.sqrt(HD))
            q_pos = own_row + lax.broadcasted_iota(jnp.int32, (n, LEN), 0) % 32
            k_pos = lax.broadcasted_iota(jnp.int32, (n, LEN), 1)
            scores = jnp.where(k_pos <= q_pos, scores, F32(-1e30))
            peak = jnp.max(scores, axis=1, keepdims=True)
            e = jnp.exp(scores - peak)
            probs = (e / jnp.sum(e, axis=1, keepdims=True)).astype(BF)
            value = jnp.dot(probs, kv[:, pl.ds(HD, HD)], preferred_element_type=F32).astype(BF)
            for h in range(n // 32):
                att[k - 1][pl.ds(own_row, 32), pl.ds((part * (n // 32) + h) * HD, HD)] = value[h * 32 : (h + 1) * 32, :]
        rows = pl.ds(own_row, 32)
        att_moves[k - 1]["z"] = [send(att[k - 1].at[rows], att[k - 1].at[rows], at_z(d)) for d in (2, 1, 3)]

    def rows_of(dg, dy, start=0, size=128):
        gg = (g + dg) % 2
        return pl.ds(pl.multiple_of(gg * 512 + ((y + dy) % 4) * 128 + start, 64), size)

    def att_y(a):
        m = att_moves[a]
        for copy in m["z"]:
            copy.wait_recv()
        rows = rows_of(0, 0)
        m["p"] = send(att[a].at[rows], att[a].at[rows], at_y(1))
        m["m"] = send(att[a].at[rows], att[a].at[rows], at_y(3))
        m["s0"] = send(att[a].at[rows], att[a].at[rows], sibling)

    def att_relay(a):
        m = att_moves[a]
        m["p"].wait_recv()
        rows = rows_of(0, 3, 0, 64)
        m["rp"] = send(att[a].at[rows], att[a].at[rows], at_y(1))
        m["m"].wait_recv()
        rows = rows_of(0, 1, 64, 64)
        m["rm"] = send(att[a].at[rows], att[a].at[rows], at_y(3))
        for name, d in (("s3", 3), ("s1", 1)):
            rows = rows_of(0, d)
            m[name] = send(att[a].at[rows], att[a].at[rows], sibling)

    def att_last(a):
        m = att_moves[a]
        m["rp"].wait_recv()
        m["rm"].wait_recv()
        rows = rows_of(0, 2)
        m["s2"] = send(att[a].at[rows], att[a].at[rows], sibling)

    def out_block(a, dg, dy):
        if dg == 1:
            att_moves[a][f"s{dy}"].wait_recv()
        rows = rows_of(dg, dy)
        value = jnp.dot(att[a][rows, :], wo[pl.ds(a * QW, QW), :], preferred_element_type=F32)
        if a == 0:
            acc[rows, :] = value
            return
        total = acc[rows, :] + value
        acc[rows, :] = total
        bsend[rows, :] = total.astype(BF)
        block = ((g + dg) % 2) * 4 + (y + dy) % 4
        index = len(branch_moves)
        copy = pltpu.make_async_remote_copy(
            src_ref=bsend.at[rows],
            dst_ref=brecv.at[c],
            send_sem=bssem.at[index],
            recv_sem=brsem.at[c],
            device_id={"col": block},
            device_id_type=MESH,
        )
        branch_moves.append((block, copy))

        @pl.when(block != c)
        def _():
            copy.start()

    branch_moves = []

    l_k.wait()
    l_v.wait()
    sib_stage(0)
    own_stage(0)
    l_q.wait()
    sib_stage(1)
    y_first(0)
    own_stage(1)
    y_second(0)
    y_first(1)
    sib_stage(2)
    z_first(0)
    y_second(1)
    own_stage(2)
    y_first(2)
    kv_finish()
    z_first(1)
    y_second(2)
    kv_y()
    queries(1)
    kv_sib()
    z_first(2)
    kv_moves["s"].wait_recv()
    attention(1)
    queries(2)
    attention(2)
    att_y(0)
    att_y(1)
    att_relay(0)
    l_o.wait()
    out_block(0, 0, 0)
    out_block(0, 1, 0)
    att_relay(1)
    att_last(0)
    out_block(0, 0, 1)
    out_block(0, 0, 3)
    out_block(0, 1, 1)
    out_block(0, 1, 3)
    out_block(1, 0, 0)
    out_block(1, 1, 0)
    out_block(0, 0, 2)
    out_block(0, 1, 2)
    out_block(1, 0, 1)
    out_block(1, 0, 3)
    out_block(1, 1, 1)
    out_block(1, 1, 3)
    att_last(1)
    out_block(1, 0, 2)
    out_block(1, 1, 2)

    upper, lower = pl.ds(0, 512), pl.ds(512, 512)
    moves_b = []
    for j in range(4):
        block = (zh - j + 4) % 4
        up = describe(panel.at[block, upper], panel.at[block, upper], at_y(1))
        down = describe(panel.at[block, lower], panel.at[block, lower], at_y(3))
        over = describe(panel.at[block], panel.at[block], sibling)
        moves_b.append((block, up, down, over))

    def panel_block(j):
        _, up, down, over = moves_b[j]

        @pl.when(is_source)
        def _():
            if j == 0:
                own_panel.wait()
            else:
                part_a[j - 1].wait_recv()

        @pl.when(jnp.logical_and(panel_core, delta != 0))
        def _():
            up.wait_recv()

        @pl.when(jnp.logical_and(panel_core, delta != 3))
        def _():
            up.start()

        @pl.when(jnp.logical_and(panel_core, delta != 0))
        def _():
            down.wait_recv()

        @pl.when(jnp.logical_and(panel_core, delta != 1))
        def _():
            down.start()

        @pl.when(panel_core)
        def _():
            over.start()

    def panel_end():
        for j, (block, up, down, over) in enumerate(moves_b):
            @pl.when(jnp.logical_and(panel_core, delta != 3))
            def _():
                up.wait_send()

            @pl.when(jnp.logical_and(panel_core, delta != 1))
            def _():
                down.wait_send()

            @pl.when(panel_core)
            def _():
                over.wait_send()

            @pl.when(jnp.logical_not(panel_core))
            def _():
                over.wait_recv()

        @pl.when(is_source)
        def _():
            for copy in part_a:
                copy.wait_send()

    panel_block(0)
    panel_block(1)

    for s in range(1, 8):
        src = (c + s) % 8
        pltpu.make_async_remote_copy(
            src_ref=bsend.at[pl.ds(0, 128)],
            dst_ref=brecv.at[src],
            send_sem=bssem.at[0],
            recv_sem=brsem.at[src],
            device_id={"col": src},
            device_id_type=MESH,
        ).wait_recv()

    def reduce_strip(i):
        r = pl.ds(pl.multiple_of(c * 128 + i, 16), 16)
        total = acc[r, :]
        for s in range(1, 8):
            total = total + brecv[(c + s) % 8, pl.ds(i, 16), :].astype(F32)
        ball[r, :] = total.astype(BF)

    strips(128, 16, reduce_strip)
    last = [send(ball.at[my_tokens], ball.at[my_tokens], at_col(*o)) for o in reversed(col_offsets)]
    panel_block(2)
    panel_block(3)
    for copy in last:
        copy.wait_recv()
    out_branch = pltpu.make_async_copy(ball, branch_out, lsem.at[len(local)])
    local.append(None)
    out_branch.start()
    panel_end()
    out_panel = pltpu.make_async_copy(panel, panel_out, lsem.at[len(local)])
    local.append(None)
    out_panel.start()
    for copy in sends:
        copy.wait_send()
    for block, copy in branch_moves:
        @pl.when(block != c)
        def _():
            copy.wait_send()

    out_tf.wait()
    out_branch.wait()
    out_panel.wait()


def scratch_shapes():
    v = pltpu.VMEM
    shapes = [
        v((LEN, FB), BF),
        v((LEN, FB), BF),
        v((LEN, 128), F32),
        v((FB, 256), BF),
        v((FB, 2 * QW), BF),
        v((2 * QW, FB), BF),
        v((32, 128), F32),
        v((32, 128), F32),
    ]
    shapes += [v((512, w), BF) for w in WIDTHS]
    shapes += [v((512, w), BF) for w in WIDTHS]
    shapes += [v((512, w), F32) for w in WIDTHS]
    for _ in range(6):
        shapes += [v((128, w), BF) for w in WIDTHS]
    shapes += [v((128, w), F32) for w in WIDTHS]
    shapes += [v((128, w), BF) for w in WIDTHS]
    shapes += [v((3, 32, w), BF) for w in WIDTHS]
    shapes += [v((LEN, 256), BF), v((32, 128), F32), v((2, 256, HD), BF)]
    shapes += [v((LEN, QW), BF)] * 2
    shapes += [v((LEN, FB), F32), v((LEN, FB), BF), v((8, 128, FB), BF), v((LEN, FB), BF), v((4, LEN, FB), BF)]
    dma = pltpu.SemaphoreType.DMA
    shapes += [dma((128,)), dma((128,)), dma((16,)), dma((8,)), dma((8,))]
    return shapes


def panel_product(left, right):
    return lax.dot_general(left, right, (((1,), (0,)), ((), ())), preferred_element_type=F32)


def per_device(tokens, norm_gain, query_weight, key_weight, value_weight, output_weight):
    cosine, sine = tables()
    anywhere = pl.BlockSpec(memory_space=pl.ANY)
    in_vmem = pl.BlockSpec(memory_space=pltpu.VMEM)
    gathered, panel, branch = pl.pallas_call(
        kernel,
        out_shape=(
            jax.ShapeDtypeStruct((LEN, FB), BF),
            jax.ShapeDtypeStruct((4, LEN, FB), BF),
            jax.ShapeDtypeStruct((LEN, FB), BF),
        ),
        in_specs=[anywhere, in_vmem] + [anywhere] * 6,
        out_specs=(anywhere,) * 3,
        scratch_shapes=scratch_shapes(),
        compiler_params=pltpu.CompilerParams(
            collective_id=0, has_side_effects=True, vmem_limit_bytes=58 * 2**20
        ),
        name="layer",
    )(
        tokens,
        norm_gain.reshape(1, FB),
        key_weight,
        value_weight,
        query_weight,
        output_weight,
        jnp.asarray(cosine),
        jnp.asarray(sine),
    )
    gram = panel_product(panel, gathered).reshape(4 * FB, FB) / LEN
    cross = panel_product(panel, branch).reshape(4 * FB, FB) / LEN
    return (gram, cross)


def solution(mesh):
    return jax.shard_map(
        per_device,
        mesh=mesh,
        in_specs=(
            P("col", ("grp", "row")),
            P(("grp", "row")),
            P(("grp", "row"), "col"),
            P(("grp", "row"), "col"),
            P(("grp", "row"), "col"),
            P("col", ("grp", "row")),
        ),
        out_specs=(P("col", ("grp", "row")), P("col", ("grp", "row"))),
        check_vma=False,
    )
```

time: 614 us -> 276 us (0.45)
  the two profiles are of different devices: /device:TPU:1 before, /device:TPU:49 now
where the time goes in v1:
time: 276 us; the launch traced here: 275 us
  Pallas kernels  262 us (95%)
  matrix products  11.4 us (4%)
    pallas_call x1, Pallas kernels, per_device(): pl.pallas_call(kernel, out_shape=(jax.ShapeDtypeStruct((LEN, FB), BF), ja...  262 us
    dot_general x2, matrix products, panel_product(): lax.dot_general(left, right, (((1,), (0,)), ((), ())), preferred_element_...  11.4 us

profile of v1, /device:TPU:49, one launch (start us, length us, event | category | flops | bytes accessed | tf_op | source)
XLA Modules:
  0.0 275.4 jit_solution(1323016159317111638)
XLA Ops:
  0.6 1.3 reshape.13.gain
  1.9 262.0 %layer.1 = (bf16[1024,512]{1,0:T(8,128)(2,1)}, bf16[4,1024,512]{2,1,0:T(8,128)(2,1)}, bf16[1024,512]{1,0:T(8,128)(2,1)}) custom-call(bf16[128,512]{1,0:T(8,128)(2,1)} %tok.1, bf16[1,512]{1,0:T(2,128)(2,1)} %reshape.13.gain, bf16[512,128]{1,0:T(8,128)(2,1)} %wk_in.1, bf16[512,128]{1,0:T(8,128)(2,1)} %wv_in.1, bf16[512,2048]{1,0:T(8,128)(2,1)} %wq_in.1, ...), custom_call_target="tpu_custom_call" | custom-call | tf_op jit(solution)/shard_map/layer/pallas_call | solution.py:581
  263.9 0.0 copy-start
  264.0 0.0 copy-start.1
  264.0 7.0 %convolution_multiply_fusion.1 = f32[4,512,512]{2,1,0:T(8,128)} fusion(bf16[4,1024,512]{2,1,0:T(8,128)(2,1)} %get-tuple-element.5, bf16[1024,512]{1,0:T(8,128)(2,1)} %get-tuple-element.6), kind=kOutput, calls=%fused_computation.1 | convolution fusion | flops 2148532224 | bytes 9437184 | tf_op jit(solution)/shard_map/dot_general | solution.py:574
  271.0 0.0 copy-done
  271.0 0.0 copy-done.1
  271.0 4.4 %convolution_multiply_fusion = f32[4,512,512]{2,1,0:T(8,128)} fusion(bf16[4,1024,512]{2,1,0:T(8,128)(2,1)S(1)} %copy-done, bf16[1024,512]{1,0:T(8,128)(2,1)S(1)} %copy-done.1), kind=kOutput, calls=%fused_computation | convolution fusion | flops 2148532224 | bytes 9437184 | tf_op jit(solution)/shard_map/dot_general | solution.py:574
Async XLA Ops:
  263.9 7.1 %copy-start = (bf16[4,1024,512]{2,1,0:T(8,128)(2,1)S(1)}, bf16[4,1024,512]{2,1,0:T(8,128)(2,1)}, u32[]{:S(2)}) copy-start(bf16[4,1024,512]{2,1,0:T(8,128)(2,1)} %get-tuple-element.5) | copy-start | bytes 12582916
  264.0 7.0 %copy-start.1 = (bf16[1024,512]{1,0:T(8,128)(2,1)S(1)}, bf16[1024,512]{1,0:T(8,128)(2,1)}, u32[]{:S(2)}) copy-start(bf16[1024,512]{1,0:T(8,128)(2,1)} %get-tuple-element.7) | copy-start | bytes 3145732

commit v2 on v1

--- a/solution.py
+++ b/solution.py
@@ -40,6 +40,21 @@
         return carry
 
     lax.fori_loop(0, rows // step, one, 0)
+
+
+class Move:
+    def __init__(self, copy):
+        self.copy, self.open = copy, True
+
+    def start(self):
+        self.copy.start()
+
+    def wait_recv(self):
+        self.open = False
+        self.copy.wait_recv()
+
+    def wait_send(self):
+        self.copy.wait_send()
 
 
 def kernel(tok, gain, wk_in, wv_in, wq_in, wo_in, cos_in, sin_in, tf_out, panel_out, branch_out, *scratch):
@@ -123,7 +138,7 @@
         )
 
     def send(src, dst, dev):
-        copy = describe(src, dst, dev)
+        copy = Move(describe(src, dst, dev))
         copy.start()
         sends.append(copy)
         return copy
@@ -136,15 +151,76 @@
     panel_core = g == c // 4
     delta = (y - c % 4 + 4) % 4
     is_source = jnp.logical_and(panel_core, delta == 0)
-    part_a = [describe(tf, panel.at[zh], at_z(d)) for d in (1, 2, 3)]
-    own_panel = pltpu.make_async_copy(tf, panel.at[zh], lsem.at[len(local)])
+
+    def quarter(d):
+        return pl.ds(pl.multiple_of(((y + d) % 4) * 256, 256), 256)
+
+    spread = [describe(tf.at[quarter(d)], panel.at[zh, quarter(d)], at_y(d)) for d in (1, 2, 3)]
+    across = [describe(panel.at[zh, quarter(0)], panel.at[zh, quarter(0)], at_z(d)) for d in (1, 2, 3)]
+    pairs = [pl.ds(0, 2), pl.ds(2, 2)]
+    along = [
+        [describe(panel.at[p, quarter(0)], panel.at[p, quarter(0)], at_y(d)) for d in (1, 3, 2)] for p in pairs
+    ]
+    over_own = describe(panel.at[:, quarter(0)], panel.at[:, quarter(0)], sibling)
+    over = [
+        [describe(panel.at[p, quarter(4 - d)], panel.at[p, quarter(4 - d)], sibling) for d in (1, 3, 2)] for p in pairs
+    ]
+    own_quarter = pltpu.make_async_copy(tf.at[quarter(0)], panel.at[zh, quarter(0)], lsem.at[len(local)])
     local.append(None)
 
     @pl.when(is_source)
     def _():
-        for copy in part_a:
+        for copy in spread:
             copy.start()
-        own_panel.start()
+        own_quarter.start()
+
+    def panel_across():
+        @pl.when(is_source)
+        def _():
+            own_quarter.wait()
+
+        for d in (1, 2, 3):
+            @pl.when(jnp.logical_and(panel_core, delta == d))
+            def _():
+                spread[d - 1].wait_recv()
+
+        @pl.when(panel_core)
+        def _():
+            for copy in across:
+                copy.start()
+
+    def panel_along(p):
+        @pl.when(panel_core)
+        def _():
+            if p == 0:
+                for copy in across:
+                    copy.wait_recv()
+                over_own.start()
+            for copy in along[p]:
+                copy.start()
+
+    def panel_over(p):
+        @pl.when(panel_core)
+        def _():
+            for copy, onward in zip(along[p], over[p]):
+                copy.wait_recv()
+                onward.start()
+
+    def panel_end():
+        @pl.when(is_source)
+        def _():
+            for copy in spread:
+                copy.wait_send()
+
+        @pl.when(panel_core)
+        def _():
+            for copy in across + along[0] + along[1] + [over_own] + over[0] + over[1]:
+                copy.wait_send()
+
+        @pl.when(jnp.logical_not(panel_core))
+        def _():
+            for copy in [over_own] + over[0] + over[1]:
+                copy.wait_recv()
 
     out_tf = pltpu.make_async_copy(tf, tf_out, lsem.at[len(local)])
     local.append(None)
@@ -295,6 +371,9 @@
             copy.wait_recv()
         rows = pl.ds(half_rows, 512)
         kv_moves["s"] = send(kv.at[rows], kv.at[rows], sibling)
+
+    def kv_here():
+        kv_moves["s"].wait_recv()
 
     att_moves = [{}, {}]
 
@@ -384,151 +463,104 @@
 
     branch_moves = []
 
-    l_k.wait()
-    l_v.wait()
-    sib_stage(0)
-    own_stage(0)
-    l_q.wait()
-    sib_stage(1)
-    y_first(0)
-    own_stage(1)
-    y_second(0)
-    y_first(1)
-    sib_stage(2)
-    z_first(0)
-    y_second(1)
-    own_stage(2)
-    y_first(2)
-    kv_finish()
-    z_first(1)
-    y_second(2)
-    kv_y()
-    queries(1)
-    kv_sib()
-    z_first(2)
-    kv_moves["s"].wait_recv()
-    attention(1)
-    queries(2)
-    attention(2)
-    att_y(0)
-    att_y(1)
-    att_relay(0)
-    l_o.wait()
-    out_block(0, 0, 0)
-    out_block(0, 1, 0)
-    att_relay(1)
-    att_last(0)
-    out_block(0, 0, 1)
-    out_block(0, 0, 3)
-    out_block(0, 1, 1)
-    out_block(0, 1, 3)
-    out_block(1, 0, 0)
-    out_block(1, 1, 0)
-    out_block(0, 0, 2)
-    out_block(0, 1, 2)
-    out_block(1, 0, 1)
-    out_block(1, 0, 3)
-    out_block(1, 1, 1)
-    out_block(1, 1, 3)
-    att_last(1)
-    out_block(1, 0, 2)
-    out_block(1, 1, 2)
-
-    upper, lower = pl.ds(0, 512), pl.ds(512, 512)
-    moves_b = []
-    for j in range(4):
-        block = (zh - j + 4) % 4
-        up = describe(panel.at[block, upper], panel.at[block, upper], at_y(1))
-        down = describe(panel.at[block, lower], panel.at[block, lower], at_y(3))
-        over = describe(panel.at[block], panel.at[block], sibling)
-        moves_b.append((block, up, down, over))
-
-    def panel_block(j):
-        _, up, down, over = moves_b[j]
-
-        @pl.when(is_source)
-        def _():
-            if j == 0:
-                own_panel.wait()
-            else:
-                part_a[j - 1].wait_recv()
-
-        @pl.when(jnp.logical_and(panel_core, delta != 0))
-        def _():
-            up.wait_recv()
-
-        @pl.when(jnp.logical_and(panel_core, delta != 3))
-        def _():
-            up.start()
-
-        @pl.when(jnp.logical_and(panel_core, delta != 0))
-        def _():
-            down.wait_recv()
-
-        @pl.when(jnp.logical_and(panel_core, delta != 1))
-        def _():
-            down.start()
-
-        @pl.when(panel_core)
-        def _():
-            over.start()
-
-    def panel_end():
-        for j, (block, up, down, over) in enumerate(moves_b):
-            @pl.when(jnp.logical_and(panel_core, delta != 3))
-            def _():
-                up.wait_send()
-
-            @pl.when(jnp.logical_and(panel_core, delta != 1))
-            def _():
-                down.wait_send()
-
-            @pl.when(panel_core)
-            def _():
-                over.wait_send()
-
-            @pl.when(jnp.logical_not(panel_core))
-            def _():
-                over.wait_recv()
-
-        @pl.when(is_source)
-        def _():
-            for copy in part_a:
-                copy.wait_send()
-
-    panel_block(0)
-    panel_block(1)
-
-    for s in range(1, 8):
-        src = (c + s) % 8
-        pltpu.make_async_remote_copy(
-            src_ref=bsend.at[pl.ds(0, 128)],
-            dst_ref=brecv.at[src],
-            send_sem=bssem.at[0],
-            recv_sem=brsem.at[src],
-            device_id={"col": src},
-            device_id_type=MESH,
-        ).wait_recv()
-
-    def reduce_strip(i):
-        r = pl.ds(pl.multiple_of(c * 128 + i, 16), 16)
-        total = acc[r, :]
+    def branch_sum():
         for s in range(1, 8):
-            total = total + brecv[(c + s) % 8, pl.ds(i, 16), :].astype(F32)
-        ball[r, :] = total.astype(BF)
-
-    strips(128, 16, reduce_strip)
-    last = [send(ball.at[my_tokens], ball.at[my_tokens], at_col(*o)) for o in reversed(col_offsets)]
-    panel_block(2)
-    panel_block(3)
-    for copy in last:
-        copy.wait_recv()
+            src = (c + s) % 8
+            pltpu.make_async_remote_copy(
+                src_ref=bsend.at[pl.ds(0, 128)],
+                dst_ref=brecv.at[src],
+                send_sem=bssem.at[0],
+                recv_sem=brsem.at[src],
+                device_id={"col": src},
+                device_id_type=MESH,
+            ).wait_recv()
+
+        def reduce_strip(i):
+            r = pl.ds(pl.multiple_of(c * 128 + i, 16), 16)
+            total = acc[r, :]
+            for s in range(1, 8):
+                total = total + brecv[(c + s) % 8, pl.ds(i, 16), :].astype(F32)
+            ball[r, :] = total.astype(BF)
+
+        strips(128, 16, reduce_strip)
+        last = [send(ball.at[my_tokens], ball.at[my_tokens], at_col(*o)) for o in reversed(col_offsets)]
+        branch_last.extend(last)
+
+    def branch_end():
+        for copy in branch_last:
+            copy.wait_recv()
+        out_branch.start()
+
+    branch_last = []
     out_branch = pltpu.make_async_copy(ball, branch_out, lsem.at[len(local)])
     local.append(None)
-    out_branch.start()
-    panel_end()
     out_panel = pltpu.make_async_copy(panel, panel_out, lsem.at[len(local)])
     local.append(None)
+
+    def loaded(*copies):
+        for copy in copies:
+            copy.wait()
+
+    plan = [
+        (loaded, l_k, l_v),
+        (sib_stage, 0),
+        (own_stage, 0),
+        (loaded, l_q),
+        (sib_stage, 1),
+        (y_first, 0),
+        (own_stage, 1),
+        (panel_across,),
+        (y_second, 0),
+        (y_first, 1),
+        (sib_stage, 2),
+        (z_first, 0),
+        (y_second, 1),
+        (own_stage, 2),
+        (y_first, 2),
+        (kv_finish,),
+        (z_first, 1),
+        (y_second, 2),
+        (kv_y,),
+        (queries, 1),
+        (kv_sib,),
+        (z_first, 2),
+        (kv_here,),
+        (panel_along, 0),
+        (attention, 1),
+        (queries, 2),
+        (att_y, 0),
+        (attention, 2),
+        (att_y, 1),
+        (att_relay, 0),
+        (loaded, l_o),
+        (out_block, 0, 0, 0),
+        (out_block, 0, 1, 0),
+        (att_relay, 1),
+        (att_last, 0),
+        (out_block, 0, 0, 1),
+        (out_block, 0, 0, 3),
+        (out_block, 0, 1, 1),
+        (out_block, 0, 1, 3),
+        (out_block, 1, 0, 0),
+        (out_block, 1, 1, 0),
+        (out_block, 0, 0, 2),
+        (out_block, 0, 1, 2),
+        (out_block, 1, 0, 1),
+        (out_block, 1, 0, 3),
+        (out_block, 1, 1, 1),
+        (out_block, 1, 1, 3),
+        (att_last, 1),
+        (panel_along, 1),
+        (out_block, 1, 0, 2),
+        (out_block, 1, 1, 2),
+        (branch_sum,),
+        (panel_over, 0),
+        (panel_over, 1),
+        (branch_end,),
+        (panel_end,),
+    ]
+    for stage, *values in plan:
+        stage(*values)
     out_panel.start()
     for copy in sends:
         copy.wait_send()

time: 276 us -> 146 us (0.53)
  the two profiles are of different devices: /device:TPU:49 before, /device:TPU:92 now
where the time goes in v2:
time: 146 us
  Pallas kernels  133 us (91%)
  matrix products  11.4 us (8%)
    pallas_call x1, Pallas kernels, per_device(): pl.pallas_call(kernel, out_shape=(jax.ShapeDtypeStruct((LEN, FB), BF), ja...  133 us
    dot_general x2, matrix products, panel_product(): lax.dot_general(left, right, (((1,), (0,)), ((), ())), preferred_element_...  11.4 us

profile of v2, /device:TPU:92, one launch (start us, length us, event | category | flops | bytes accessed | tf_op | source)
XLA Modules:
  0.0 146.1 jit_solution(15277082249181426221)
XLA Ops:
  0.6 1.3 reshape.13.gain
  1.9 132.7 %layer.1 = (bf16[1024,512]{1,0:T(8,128)(2,1)}, bf16[4,1024,512]{2,1,0:T(8,128)(2,1)}, bf16[1024,512]{1,0:T(8,128)(2,1)}) custom-call(bf16[128,512]{1,0:T(8,128)(2,1)} %tok.1, bf16[1,512]{1,0:T(2,128)(2,1)} %reshape.13.gain, bf16[512,128]{1,0:T(8,128)(2,1)} %wk_in.1, bf16[512,128]{1,0:T(8,128)(2,1)} %wv_in.1, bf16[512,2048]{1,0:T(8,128)(2,1)} %wq_in.1, ...), custom_call_target="tpu_custom_call" | custom-call | tf_op jit(solution)/shard_map/layer/pallas_call | solution.py:613
  134.6 0.0 copy-start
  134.6 0.0 copy-start.1
  134.6 7.0 %convolution_multiply_fusion.1 = f32[4,512,512]{2,1,0:T(8,128)} fusion(bf16[4,1024,512]{2,1,0:T(8,128)(2,1)} %get-tuple-element.5, bf16[1024,512]{1,0:T(8,128)(2,1)} %get-tuple-element.6), kind=kOutput, calls=%fused_computation.1 | convolution fusion | flops 2148532224 | bytes 9437184 | tf_op jit(solution)/shard_map/dot_general | solution.py:606
  141.7 0.0 copy-done
  141.7 0.0 copy-done.1
  141.7 4.4 %convolution_multiply_fusion = f32[4,512,512]{2,1,0:T(8,128)} fusion(bf16[4,1024,512]{2,1,0:T(8,128)(2,1)S(1)} %copy-done, bf16[1024,512]{1,0:T(8,128)(2,1)S(1)} %copy-done.1), kind=kOutput, calls=%fused_computation | convolution fusion | flops 2148532224 | bytes 9437184 | tf_op jit(solution)/shard_map/dot_general | solution.py:606
Async XLA Ops:
  134.6 7.1 %copy-start = (bf16[4,1024,512]{2,1,0:T(8,128)(2,1)S(1)}, bf16[4,1024,512]{2,1,0:T(8,128)(2,1)}, u32[]{:S(2)}) copy-start(bf16[4,1024,512]{2,1,0:T(8,128)(2,1)} %get-tuple-element.5) | copy-start | bytes 12582916
  134.6 7.0 %copy-start.1 = (bf16[1024,512]{1,0:T(8,128)(2,1)S(1)}, bf16[1024,512]{1,0:T(8,128)(2,1)}, u32[]{:S(2)}) copy-start(bf16[1024,512]{1,0:T(8,128)(2,1)} %get-tuple-element.7) | copy-start | bytes 3145732

commit v3 on v2

--- a/solution.py
+++ b/solution.py
@@ -73,7 +73,7 @@
     s2 = [nxt() for _ in range(3)]
     z_send = [nxt() for _ in range(3)]
     z_recv = [nxt() for _ in range(3)]
-    kv, rs_scale, qs = [nxt() for _ in range(3)]
+    kv, rs_scale, qs, bias = [nxt() for _ in range(4)]
     att = [nxt() for _ in range(2)]
     acc, bsend, brecv, ball, panel = [nxt() for _ in range(5)]
     ssem, rsem, lsem, bssem, brsem = [nxt() for _ in range(5)]
@@ -105,13 +105,14 @@
         return copy
 
     own_row = pl.multiple_of(g * 512 + y * 128 + zh * 32, 32)
+    first_token = pl.multiple_of(((g * 4 + y + c) % 8) * 128 + zh * 32, 32)
     my_tokens = pl.ds(pl.multiple_of(c * 128, 128), 128)
     l_tok = load(tok, tf.at[my_tokens])
     l_k = load(wk_in, wkv.at[:, pl.ds(0, HD)])
     l_v = load(wv_in, wkv.at[:, pl.ds(HD, HD)])
     l_q = load(wq_in, wq)
-    l_cos = load(cos_in.at[pl.ds(own_row, 32)], cosv)
-    l_sin = load(sin_in.at[pl.ds(own_row, 32)], sinv)
+    l_cos = load(cos_in.at[pl.ds(first_token, 32)], cosv)
+    l_sin = load(sin_in.at[pl.ds(first_token, 32)], sinv)
     l_o = load(wo_in, wo)
 
     barrier = pltpu.get_barrier_semaphore()
@@ -144,9 +145,10 @@
         return copy
 
     gather = [send(tok, tf.at[my_tokens], at_col(*o)) for o in col_offsets]
-    l_tok.wait()
-    for copy in gather:
-        copy.wait_recv()
+    positions = first_token + lax.broadcasted_iota(jnp.int32, (32, 128), 0)
+    for v in range(8):
+        keys_at = ((v + c) % 8) * 128 + lax.broadcasted_iota(jnp.int32, (32, 128), 1)
+        bias[:, v * 128 : (v + 1) * 128] = jnp.where(keys_at <= positions, F32(0), F32(-1e30))
 
     panel_core = g == c // 4
     delta = (y - c % 4 + 4) % 4
@@ -157,22 +159,22 @@
 
     spread = [describe(tf.at[quarter(d)], panel.at[zh, quarter(d)], at_y(d)) for d in (1, 2, 3)]
     across = [describe(panel.at[zh, quarter(0)], panel.at[zh, quarter(0)], at_z(d)) for d in (1, 2, 3)]
-    pairs = [pl.ds(0, 2), pl.ds(2, 2)]
-    along = [
-        [describe(panel.at[p, quarter(0)], panel.at[p, quarter(0)], at_y(d)) for d in (1, 3, 2)] for p in pairs
+    along = [describe(panel.at[:, quarter(0)], panel.at[:, quarter(0)], at_y(d)) for d in (1, 3)]
+    relays = [
+        describe(panel.at[p, quarter(d)], panel.at[p, quarter(d)], at_y(4 - d)) for p, d in ((pl.ds(0, 2), 3), (pl.ds(2, 2), 1))
     ]
-    over_own = describe(panel.at[:, quarter(0)], panel.at[:, quarter(0)], sibling)
-    over = [
-        [describe(panel.at[p, quarter(4 - d)], panel.at[p, quarter(4 - d)], sibling) for d in (1, 3, 2)] for p in pairs
-    ]
+    over = [describe(panel.at[:, quarter(d)], panel.at[:, quarter(d)], sibling) for d in (0, 3, 1, 2)]
     own_quarter = pltpu.make_async_copy(tf.at[quarter(0)], panel.at[zh, quarter(0)], lsem.at[len(local)])
     local.append(None)
 
-    @pl.when(is_source)
-    def _():
-        for copy in spread:
-            copy.start()
-        own_quarter.start()
+    def panel_spread():
+        out_tf.start()
+
+        @pl.when(is_source)
+        def _():
+            for copy in spread:
+                copy.start()
+            own_quarter.start()
 
     def panel_across():
         @pl.when(is_source)
@@ -189,22 +191,30 @@
             for copy in across:
                 copy.start()
 
-    def panel_along(p):
+    def panel_along():
         @pl.when(panel_core)
         def _():
-            if p == 0:
-                for copy in across:
-                    copy.wait_recv()
-                over_own.start()
-            for copy in along[p]:
+            for copy in across:
+                copy.wait_recv()
+            for copy in along:
                 copy.start()
-
-    def panel_over(p):
+            over[0].start()
+
+    def panel_relay():
         @pl.when(panel_core)
         def _():
-            for copy, onward in zip(along[p], over[p]):
+            for i in range(2):
+                along[i].wait_recv()
+                relays[i].start()
+            over[1].start()
+            over[2].start()
+
+    def panel_last():
+        @pl.when(panel_core)
+        def _():
+            for copy in relays:
                 copy.wait_recv()
-                onward.start()
+            over[3].start()
 
     def panel_end():
         @pl.when(is_source)
@@ -214,53 +224,70 @@
 
         @pl.when(panel_core)
         def _():
-            for copy in across + along[0] + along[1] + [over_own] + over[0] + over[1]:
+            for copy in across + along + relays + over:
                 copy.wait_send()
 
         @pl.when(jnp.logical_not(panel_core))
         def _():
-            for copy in [over_own] + over[0] + over[1]:
+            for copy in over:
                 copy.wait_recv()
 
     out_tf = pltpu.make_async_copy(tf, tf_out, lsem.at[len(local)])
     local.append(None)
-    out_tf.start()
-
-    def prepare(i):
-        rows = pl.ds(i, 32)
-        wide = tf[rows, :].astype(F32)
-        xg[rows, :] = (wide * gain[...].astype(F32)).astype(BF)
-        square = wide * wide
-        sq[rows, :] = square[:, 0:128] + square[:, 128:256] + square[:, 256:384] + square[:, 384:512]
-
-    strips(LEN, 32, prepare)
-
-    mine = pl.multiple_of(g * 512, 512)
-    theirs = pl.multiple_of((1 - g) * 512, 512)
-
-    def project(k, base, out):
-        weights, first, wide = (wkv, 0, 256) if k == 0 else (wq, (k - 1) * QW, QW)
-
-        def tile(i):
-            value = jnp.dot(
-                xg[pl.ds(base, 512), :],
-                weights[:, pl.ds(pl.multiple_of(first + i, 256), 256)],
-                preferred_element_type=F32,
-            )
-            out[:, pl.ds(i, 256)] = value.astype(out.dtype)
-
-        strips(wide, 256, tile)
-        if k == 0:
-            out[:, pl.ds(256, 128)] = sq[pl.ds(base, 512), :].astype(out.dtype)
-
-    sib = [None] * 3
-
-    def sib_stage(k):
-        project(k, theirs, sib_send[k])
-        sib[k] = send(sib_send[k], sib_recv[k], sibling)
-
-    def own_stage(k):
-        project(k, mine, r1[k])
+
+    sib = [[], [], []]
+
+    def arrive(i):
+        dx, dl = ((0, 0), *col_offsets)[i]
+        if i == 0:
+            l_tok.wait()
+        else:
+            gather[i - 1].wait_recv()
+        block = ((x + 4 - dx) % 4) * 2 + (zl + dl) % 2
+        base = pl.multiple_of(block * 128, 128)
+        slot = (block + 8 - c) % 8
+        here = slot // 4 == g
+        part = pl.ds(pl.multiple_of((slot % 4) * 128, 128), 128)
+
+        def prepare(j):
+            rows = pl.ds(pl.multiple_of(base + j, 32), 32)
+            wide = tf[rows, :].astype(F32)
+            xg[rows, :] = (wide * gain[...].astype(F32)[None, :]).astype(BF)
+            square = wide * wide
+            sq[rows, :] = square[:, 0:128] + square[:, 128:256] + square[:, 256:384] + square[:, 384:512]
+
+        strips(128, 32, prepare)
+
+        rows = pl.ds(base, 128)
+        for k in range(3):
+            def project(out):
+                weights = wkv[...] if k == 0 else wq[:, (k - 1) * QW : k * QW]
+                wide = weights.shape[1]
+                out[part, 0:wide] = jnp.dot(xg[rows, :], weights, preferred_element_type=F32).astype(out.dtype)
+                if k == 0:
+                    out[part, 256:384] = sq[rows, :].astype(out.dtype)
+
+            @pl.when(here)
+            def _():
+                project(r1[k])
+
+            @pl.when(jnp.logical_not(here))
+            def _():
+                project(sib_send[k])
+
+            copy = describe(sib_send[k].at[part], sib_recv[k].at[part], sibling)
+            sib[k].append((here, copy))
+
+            @pl.when(jnp.logical_not(here))
+            def _():
+                copy.start()
+
+    def sib_end():
+        for moves in sib:
+            for here, copy in moves:
+                @pl.when(jnp.logical_not(here))
+                def _():
+                    copy.wait_send()
 
     def y_rows(d):
         return pl.multiple_of(((y + d) % 4) * 128, 128)
@@ -268,7 +295,11 @@
     y_moves = [None] * 3
 
     def y_first(k):
-        sib[k].wait_recv()
+        for here, copy in sib[k]:
+            @pl.when(here)
+            def _():
+                copy.wait_recv()
+
 
         def pair(d, dst, start, rows):
             base = y_rows(d)
@@ -385,17 +416,15 @@
             qs[k - 1, pl.ds(h * 32, 32), :] = rotated(value).astype(BF)
 
     def attention(k):
-        n = 128
+        n = 256
         for part in range(256 // n):
             scores = lax.dot_general(
                 qs[k - 1, pl.ds(part * n, n), :], kv[:, pl.ds(0, HD)], (((1,), (1,)), ((), ())), preferred_element_type=F32
             ) * (1.0 / math.sqrt(HD))
-            q_pos = own_row + lax.broadcasted_iota(jnp.int32, (n, LEN), 0) % 32
-            k_pos = lax.broadcasted_iota(jnp.int32, (n, LEN), 1)
-            scores = jnp.where(k_pos <= q_pos, scores, F32(-1e30))
+            scores = (scores.reshape(n // 32, 32, LEN) + bias[...][None]).reshape(n, LEN)
             peak = jnp.max(scores, axis=1, keepdims=True)
             e = jnp.exp(scores - peak)
-            probs = (e / jnp.sum(e, axis=1, keepdims=True)).astype(BF)
+            probs = (e * (1.0 / jnp.sum(e, axis=1, keepdims=True))).astype(BF)
             value = jnp.dot(probs, kv[:, pl.ds(HD, HD)], preferred_element_type=F32).astype(BF)
             for h in range(n // 32):
                 att[k - 1][pl.ds(own_row, 32), pl.ds((part * (n // 32) + h) * HD, HD)] = value[h * 32 : (h + 1) * 32, :]
@@ -452,12 +481,12 @@
             dst_ref=brecv.at[c],
             send_sem=bssem.at[index],
             recv_sem=brsem.at[c],
-            device_id={"col": block},
+            device_id={"col": (block + c) % 8},
             device_id_type=MESH,
         )
         branch_moves.append((block, copy))
 
-        @pl.when(block != c)
+        @pl.when(block != 0)
         def _():
             copy.start()
 
@@ -477,7 +506,7 @@
 
         def reduce_strip(i):
             r = pl.ds(pl.multiple_of(c * 128 + i, 16), 16)
-            total = acc[r, :]
+            total = acc[pl.ds(i, 16), :]
             for s in range(1, 8):
                 total = total + brecv[(c + s) % 8, pl.ds(i, 16), :].astype(F32)
             ball[r, :] = total.astype(BF)
@@ -502,21 +531,16 @@
             copy.wait()
 
     plan = [
-        (loaded, l_k, l_v),
-        (sib_stage, 0),
-        (own_stage, 0),
-        (loaded, l_q),
-        (sib_stage, 1),
+        (loaded, l_k, l_v, l_q),
+        *[(arrive, i) for i in range(8)],
+        (panel_spread,),
         (y_first, 0),
-        (own_stage, 1),
+        (y_first, 1),
+        (y_second, 0),
+        (y_first, 2),
+        (z_first, 0),
         (panel_across,),
-        (y_second, 0),
-        (y_first, 1),
-        (sib_stage, 2),
-        (z_first, 0),
         (y_second, 1),
-        (own_stage, 2),
-        (y_first, 2),
         (kv_finish,),
         (z_first, 1),
         (y_second, 2),
@@ -525,39 +549,39 @@
         (kv_sib,),
         (z_first, 2),
         (kv_here,),
-        (panel_along, 0),
+        (panel_along,),
         (attention, 1),
         (queries, 2),
         (att_y, 0),
         (attention, 2),
         (att_y, 1),
-        (att_relay, 0),
         (loaded, l_o),
         (out_block, 0, 0, 0),
+        (out_block, 1, 0, 0),
         (out_block, 0, 1, 0),
-        (att_relay, 1),
-        (att_last, 0),
+        (att_relay, 0),
+        (out_block, 1, 1, 0),
         (out_block, 0, 0, 1),
         (out_block, 0, 0, 3),
+        (att_relay, 1),
+        (out_block, 1, 0, 1),
+        (out_block, 1, 0, 3),
         (out_block, 0, 1, 1),
         (out_block, 0, 1, 3),
-        (out_block, 1, 0, 0),
-        (out_block, 1, 1, 0),
+        (att_last, 0),
+        (out_block, 1, 1, 1),
+        (out_block, 1, 1, 3),
         (out_block, 0, 0, 2),
         (out_block, 0, 1, 2),
-        (out_block, 1, 0, 1),
-        (out_block, 1, 0, 3),
-        (out_block, 1, 1, 1),
-        (out_block, 1, 1, 3),
         (att_last, 1),
-        (panel_along, 1),
         (out_block, 1, 0, 2),
         (out_block, 1, 1, 2),
+        (panel_relay,),
         (branch_sum,),
-        (panel_over, 0),
-        (panel_over, 1),
+        (panel_last,),
         (branch_end,),
         (panel_end,),
+        (sib_end,),
     ]
     for stage, *values in plan:
         stage(*values)
@@ -565,7 +589,7 @@
     for copy in sends:
         copy.wait_send()
     for block, copy in branch_moves:
-        @pl.when(block != c)
+        @pl.when(block != 0)
         def _():
             copy.wait_send()
 
@@ -594,16 +618,32 @@
     shapes += [v((128, w), F32) for w in WIDTHS]
     shapes += [v((128, w), BF) for w in WIDTHS]
     shapes += [v((3, 32, w), BF) for w in WIDTHS]
-    shapes += [v((LEN, 256), BF), v((32, 128), F32), v((2, 256, HD), BF)]
+    shapes += [v((LEN, 256), BF), v((32, 128), F32), v((2, 256, HD), BF), v((32, LEN), F32)]
     shapes += [v((LEN, QW), BF)] * 2
     shapes += [v((LEN, FB), F32), v((LEN, FB), BF), v((8, 128, FB), BF), v((LEN, FB), BF), v((4, LEN, FB), BF)]
     dma = pltpu.SemaphoreType.DMA
-    shapes += [dma((128,)), dma((128,)), dma((16,)), dma((8,)), dma((8,))]
+    shapes += [dma((160,)), dma((160,)), dma((16,)), dma((8,)), dma((8,))]
     return shapes
 
 
-def panel_product(left, right):
-    return lax.dot_general(left, right, (((1,), (0,)), ((), ())), preferred_element_type=F32)
+def product_kernel(panel, gathered, branch, gram, cross):
+    for right, out in ((gathered, gram), (branch, cross)):
+        out[...] = lax.dot_general(
+            panel[0], right[...], (((0,), (0,)), ((), ())), preferred_element_type=F32
+        ) * (1.0 / LEN)
+
+
+def products(panel, gathered, branch):
+    whole = pl.BlockSpec((LEN, FB), lambda i: (0, 0))
+    return pl.pallas_call(
+        product_kernel,
+        grid=(4,),
+        out_shape=(jax.ShapeDtypeStruct((4 * FB, FB), F32),) * 2,
+        in_specs=[pl.BlockSpec((1, LEN, FB), lambda i: (i, 0, 0)), whole, whole],
+        out_specs=(pl.BlockSpec((FB, FB), lambda i: (i, 0)),) * 2,
+        compiler_params=pltpu.CompilerParams(vmem_limit_bytes=60 * 2**20),
+        name="products",
+    )(panel, gathered, branch)
 
 
 def per_device(tokens, norm_gain, query_weight, key_weight, value_weight, output_weight):
@@ -626,7 +666,7 @@
         name="layer",
     )(
         tokens,
-        norm_gain.reshape(1, FB),
+        norm_gain,
         key_weight,
         value_weight,
         query_weight,
@@ -634,9 +674,7 @@
         jnp.asarray(cosine),
         jnp.asarray(sine),
     )
-    gram = panel_product(panel, gathered).reshape(4 * FB, FB) / LEN
-    cross = panel_product(panel, branch).reshape(4 * FB, FB) / LEN
-    return (gram, cross)
+    return products(panel, gathered, branch)
 
 
 def solution(mesh):

time: 146 us -> 141 us (0.966)
  the two profiles are of different devices: /device:TPU:92 before, /device:TPU:1 now
where the time goes in v3:
time: 141 us; the launch traced here: 140 us
  Pallas kernels  139 us (99%)
    pallas_call x1, Pallas kernels, per_device(): pl.pallas_call(kernel, out_shape=(jax.ShapeDtypeStruct((LEN, FB), BF), ja...  131 us
    pallas_call x1, Pallas kernels, products(): pl.pallas_call(product_kernel, grid=(4,), out_shape=(jax.ShapeDtypeStruct...  8.39 us

profile of v3, /device:TPU:1, one launch (start us, length us, event | category | flops | bytes accessed | tf_op | source)
XLA Modules:
  0.0 139.7 jit_solution(16846120222233799221)
XLA Ops:
  0.6 130.6 %layer.1 = (bf16[1024,512]{1,0:T(8,128)(2,1)}, bf16[4,1024,512]{2,1,0:T(8,128)(2,1)}, bf16[1024,512]{1,0:T(8,128)(2,1)}) custom-call(bf16[128,512]{1,0:T(8,128)(2,1)} %tok.1, bf16[512]{0:T(512)(128)(2,1)} %gain.1, bf16[512,128]{1,0:T(8,128)(2,1)} %wk_in.1, bf16[512,128]{1,0:T(8,128)(2,1)} %wv_in.1, bf16[512,2048]{1,0:T(8,128)(2,1)} %wq_in.1, ...), custom_call_target="tpu_custom_call" | custom-call | tf_op jit(solution)/shard_map/layer/pallas_call | solution.py:653
  131.3 8.4 %products.1 = (f32[2048,512]{1,0:T(8,128)}, f32[2048,512]{1,0:T(8,128)}) custom-call(bf16[4,1024,512]{2,1,0:T(8,128)(2,1)} %get-tuple-element.5.panel, bf16[1024,512]{1,0:T(8,128)(2,1)} %get-tuple-element.6.gathered, bf16[1024,512]{1,0:T(8,128)(2,1)} %get-tuple-element.7.branch), custom_call_target="tpu_custom_call" | custom-call | tf_op jit(solution)/shard_map/products/pallas_call | solution.py:638

commit v4 on v3

--- a/solution.py
+++ b/solution.py
@@ -533,13 +533,11 @@
     plan = [
         (loaded, l_k, l_v, l_q),
         *[(arrive, i) for i in range(8)],
-        (panel_spread,),
         (y_first, 0),
         (y_first, 1),
         (y_second, 0),
         (y_first, 2),
         (z_first, 0),
-        (panel_across,),
         (y_second, 1),
         (kv_finish,),
         (z_first, 1),
@@ -549,12 +547,13 @@
         (kv_sib,),
         (z_first, 2),
         (kv_here,),
-        (panel_along,),
+        (panel_spread,),
         (attention, 1),
         (queries, 2),
         (att_y, 0),
         (attention, 2),
         (att_y, 1),
+        (panel_across,),
         (loaded, l_o),
         (out_block, 0, 0, 0),
         (out_block, 1, 0, 0),
@@ -573,11 +572,12 @@
         (out_block, 1, 1, 3),
         (out_block, 0, 0, 2),
         (out_block, 0, 1, 2),
+        (panel_along,),
         (att_last, 1),
         (out_block, 1, 0, 2),
         (out_block, 1, 1, 2),
+        (branch_sum,),
         (panel_relay,),
-        (branch_sum,),
         (panel_last,),
         (branch_end,),
         (panel_end,),

time: 141 us -> 132 us (0.936)
  Pallas kernels: 139 us -> 131 us
    pallas_call x1, Pallas kernels: 131 us -> 122 us  [per_device(): pl.pallas_call(kernel, out_shape=(jax.ShapeDtypeStruct((LEN, FB), BF), ja...]
where the time goes in v4:
time: 132 us; the launch traced here: 131 us
  Pallas kernels  131 us (99%)
    pallas_call x1, Pallas kernels, per_device(): pl.pallas_call(kernel, out_shape=(jax.ShapeDtypeStruct((LEN, FB), BF), ja...  122 us
    pallas_call x1, Pallas kernels, products(): pl.pallas_call(product_kernel, grid=(4,), out_shape=(jax.ShapeDtypeStruct...  8.4 us

profile of v4, /device:TPU:1, one launch (start us, length us, event | category | flops | bytes accessed | tf_op | source)
XLA Modules:
  0.0 131.4 jit_solution(13592774818417694260)
XLA Ops:
  0.6 122.4 %layer.1 = (bf16[1024,512]{1,0:T(8,128)(2,1)}, bf16[4,1024,512]{2,1,0:T(8,128)(2,1)}, bf16[1024,512]{1,0:T(8,128)(2,1)}) custom-call(bf16[128,512]{1,0:T(8,128)(2,1)} %tok.1, bf16[512]{0:T(512)(128)(2,1)} %gain.1, bf16[512,128]{1,0:T(8,128)(2,1)} %wk_in.1, bf16[512,128]{1,0:T(8,128)(2,1)} %wv_in.1, bf16[512,2048]{1,0:T(8,128)(2,1)} %wq_in.1, ...), custom_call_target="tpu_custom_call" | custom-call | tf_op jit(solution)/shard_map/layer/pallas_call | solution.py:653
  123.0 8.4 %products.1 = (f32[2048,512]{1,0:T(8,128)}, f32[2048,512]{1,0:T(8,128)}) custom-call(bf16[4,1024,512]{2,1,0:T(8,128)(2,1)} %get-tuple-element.5.panel, bf16[1024,512]{1,0:T(8,128)(2,1)} %get-tuple-element.6.gathered, bf16[1024,512]{1,0:T(8,128)(2,1)} %get-tuple-element.7.branch), custom_call_target="tpu_custom_call" | custom-call | tf_op jit(solution)/shard_map/products/pallas_call | solution.py:638

commit v5 on v4

--- a/solution.py
+++ b/solution.py
@@ -216,6 +216,22 @@
                 copy.wait_recv()
             over[3].start()
 
+    out_parts = []
+    for d in (0, 3, 1, 2):
+        out_parts.append(
+            pltpu.make_async_copy(panel.at[:, quarter(d)], panel_out.at[:, quarter(d)], lsem.at[len(local)])
+        )
+        local.append(None)
+
+    def panel_write():
+        @pl.when(jnp.logical_not(panel_core))
+        def _():
+            for copy in over[:3]:
+                copy.wait_recv()
+
+        for copy in out_parts[:3]:
+            copy.start()
+
     def panel_end():
         @pl.when(is_source)
         def _():
@@ -229,8 +245,7 @@
 
         @pl.when(jnp.logical_not(panel_core))
         def _():
-            for copy in over:
-                copy.wait_recv()
+            over[3].wait_recv()
 
     out_tf = pltpu.make_async_copy(tf, tf_out, lsem.at[len(local)])
     local.append(None)
@@ -523,9 +538,6 @@
     branch_last = []
     out_branch = pltpu.make_async_copy(ball, branch_out, lsem.at[len(local)])
     local.append(None)
-    out_panel = pltpu.make_async_copy(panel, panel_out, lsem.at[len(local)])
-    local.append(None)
-
     def loaded(*copies):
         for copy in copies:
             copy.wait()
@@ -579,13 +591,14 @@
         (branch_sum,),
         (panel_relay,),
         (panel_last,),
+        (panel_write,),
         (branch_end,),
         (panel_end,),
         (sib_end,),
     ]
     for stage, *values in plan:
         stage(*values)
-    out_panel.start()
+    out_parts[3].start()
     for copy in sends:
         copy.wait_send()
     for block, copy in branch_moves:
@@ -595,7 +608,8 @@
 
     out_tf.wait()
     out_branch.wait()
-    out_panel.wait()
+    for copy in out_parts:
+        copy.wait()
 
 
 def scratch_shapes():

time: 132 us -> 131 us (level)
  no operation moved by 1% of the time
where the time goes in v5:
time: 131 us; the launch traced here: 130 us
  Pallas kernels  130 us (99%)
    pallas_call x1, Pallas kernels, per_device(): pl.pallas_call(kernel, out_shape=(jax.ShapeDtypeStruct((LEN, FB), BF), ja...  121 us
    pallas_call x1, Pallas kernels, products(): pl.pallas_call(product_kernel, grid=(4,), out_shape=(jax.ShapeDtypeStruct...  8.39 us

profile of v5, /device:TPU:1, one launch (start us, length us, event | category | flops | bytes accessed | tf_op | source)
XLA Modules:
  0.0 130.4 jit_solution(1149444189735628622)
XLA Ops:
  0.6 121.4 %layer.1 = (bf16[1024,512]{1,0:T(8,128)(2,1)}, bf16[4,1024,512]{2,1,0:T(8,128)(2,1)}, bf16[1024,512]{1,0:T(8,128)(2,1)}) custom-call(bf16[128,512]{1,0:T(8,128)(2,1)} %tok.1, bf16[512]{0:T(512)(128)(2,1)} %gain.1, bf16[512,128]{1,0:T(8,128)(2,1)} %wk_in.1, bf16[512,128]{1,0:T(8,128)(2,1)} %wv_in.1, bf16[512,2048]{1,0:T(8,128)(2,1)} %wq_in.1, ...), custom_call_target="tpu_custom_call" | custom-call | tf_op jit(solution)/shard_map/layer/pallas_call | solution.py:667
  122.1 8.4 %products.1 = (f32[2048,512]{1,0:T(8,128)}, f32[2048,512]{1,0:T(8,128)}) custom-call(bf16[4,1024,512]{2,1,0:T(8,128)(2,1)} %get-tuple-element.5.panel, bf16[1024,512]{1,0:T(8,128)(2,1)} %get-tuple-element.6.gathered, bf16[1024,512]{1,0:T(8,128)(2,1)} %get-tuple-element.7.branch), custom_call_target="tpu_custom_call" | custom-call | tf_op jit(solution)/shard_map/products/pallas_call | solution.py:652

commit v6 on v5

--- a/solution.py
+++ b/solution.py
@@ -144,7 +144,7 @@
         sends.append(copy)
         return copy
 
-    gather = [send(tok, tf.at[my_tokens], at_col(*o)) for o in col_offsets]
+    gather = [send(tok, tf.at[my_tokens], at_col(*o)) for o in reversed(col_offsets)][::-1]
     positions = first_token + lax.broadcasted_iota(jnp.int32, (32, 128), 0)
     for v in range(8):
         keys_at = ((v + c) % 8) * 128 + lax.broadcasted_iota(jnp.int32, (32, 128), 1)

time: 131 us -> 133 us (1.015)
  Pallas kernels: 130 us -> 133 us
    pallas_call x1, Pallas kernels: 121 us -> 124 us  [per_device(): pl.pallas_call(kernel, out_shape=(jax.ShapeDtypeStruct((LEN, FB), BF), ja...]
where the time goes in v6:
time: 133 us
  Pallas kernels  133 us (100%)
    pallas_call x1, Pallas kernels, per_device(): pl.pallas_call(kernel, out_shape=(jax.ShapeDtypeStruct((LEN, FB), BF), ja...  124 us
    pallas_call x1, Pallas kernels, products(): pl.pallas_call(product_kernel, grid=(4,), out_shape=(jax.ShapeDtypeStruct...  8.4 us

profile of v6, /device:TPU:1, one launch (start us, length us, event | category | flops | bytes accessed | tf_op | source)
XLA Modules:
  0.0 133.3 jit_solution(15060379771486512762)
XLA Ops:
  0.6 124.3 %layer.1 = (bf16[1024,512]{1,0:T(8,128)(2,1)}, bf16[4,1024,512]{2,1,0:T(8,128)(2,1)}, bf16[1024,512]{1,0:T(8,128)(2,1)}) custom-call(bf16[128,512]{1,0:T(8,128)(2,1)} %tok.1, bf16[512]{0:T(512)(128)(2,1)} %gain.1, bf16[512,128]{1,0:T(8,128)(2,1)} %wk_in.1, bf16[512,128]{1,0:T(8,128)(2,1)} %wv_in.1, bf16[512,2048]{1,0:T(8,128)(2,1)} %wq_in.1, ...), custom_call_target="tpu_custom_call" | custom-call | tf_op jit(solution)/shard_map/layer/pallas_call | solution.py:667
  124.9 8.4 %products.1 = (f32[2048,512]{1,0:T(8,128)}, f32[2048,512]{1,0:T(8,128)}) custom-call(bf16[4,1024,512]{2,1,0:T(8,128)(2,1)} %get-tuple-element.5.panel, bf16[1024,512]{1,0:T(8,128)(2,1)} %get-tuple-element.6.gathered, bf16[1024,512]{1,0:T(8,128)(2,1)} %get-tuple-element.7.branch), custom_call_target="tpu_custom_call" | custom-call | tf_op jit(solution)/shard_map/products/pallas_call | solution.py:652
